TPU v7x, 32 devices: a whole 2x2x4 slice. The times are simulated.
32 devices in a mesh: groups: 2 (over x), side: 2 (over core), dev: 8 (over z, y).
Axes of the slice: x: 2, y: 2, z: 4, core: 2. Of those that a mesh axis runs over, the one named last changes fastest.
Arguments:
- queries: bfloat16 [256, 8192], P(('groups', 'side', 'dev')), parts along dimension 0, may hold values from -7 to 7
- kv_cache: bfloat16 [1408, 16, 1024], P(('groups', 'side', 'dev')), parts along dimension 0, may hold values from -6 to 6
- new_kv: bfloat16 [256, 1024], P(('groups', 'side', 'dev')), parts along dimension 0, may hold values from -6 to 6
- lengths: int32 [256], P(('groups', 'side', 'dev')), parts along dimension 0, may hold values from 1 to 256, as said below
- page_table: int32 [256, 16], P(('groups', 'side', 'dev')), parts along dimension 0, may hold values from 0 to 43, as said below
- hidden: bfloat16 [256, 4096], P(('groups', 'side', 'dev')), parts along dimension 0, may hold values from -6 to 6
- norm_gain: float32 [4096], replicated, may hold values from 0.5 to 1.5
- route_ids: int32 [256, 8], P(('groups', 'side', 'dev')), parts along dimension 0, may hold values from 0 to 31, all different within a row; in each aligned block of 8 rows (0 to 7, 8 to 15, ...) at most 4 rows name the same one
- route_weights: float32 [256, 8], P(('groups', 'side', 'dev')), parts along dimension 0, may hold values from 0.05 to 1
- gate_w: bfloat16 [4096, 49152], P(None, ('side', 'dev')), may hold values from -0.09375 to 0.09375
- up_w: bfloat16 [4096, 49152], P(None, ('side', 'dev')), may hold values from -0.09375 to 0.09375
- down_w: bfloat16 [49152, 4096], P(('side', 'dev')), may hold values from -0.15625 to 0.15625
Outputs:
- context: bfloat16 [256, 8192], P(('groups', 'side', 'dev')), parts along dimension 0
- moe_out: bfloat16 [256, 4096], P(('groups', 'side', 'dev')), parts along dimension 0
There are 2 independent parts, one for each index of `groups`. A program takes and returns all parts, laid end to end along the dimension named above; an argument that names none is the same for every part. Nothing has to cross between parts.
Inputs may be any that keep to these rules, and one draw needn't show every extreme that they name: `route_ids`: within the rows of one device, no expert is named by more than 4 routes, a bound that some block reaches. `lengths`: of each device's 8 sequences one holds exactly 256 positions, the others at most 64. `page_table`: entries index the device's own pool of 44 pages; the first ceil(lengths / 16) entries of a row hold its positions in order and are distinct over all of the device's sequences; later entries are arbitrary.
All inputs are finite; a program needn't handle non-finite values.
Results may differ from a plain program's by a relative error of at most 0.0071.
Values may be sent and summed in bfloat16 or wider, within the bound.
A program may use at most 256 MiB of HBM per device.

v0:
```python
import jax
import jax.numpy as jnp
from jax import lax
from jax.sharding import PartitionSpec as P

D = 4096
FF = 1536
HEADS = 64
KV_HEADS = 4
HEAD_DIM = 128
TOP = 8
EXPERTS = 32
PAGE = 16
MAXP = 16
MOST = 4


eps = 1e-06


def attend_block(queries, cache_pool, page_table, lengths, new_kv):
    seq_count = queries.shape[0]
    groups = HEADS // KV_HEADS
    width_kv = 2 * KV_HEADS * HEAD_DIM
    paged = cache_pool[page_table].reshape(seq_count, MAXP * PAGE, width_kv)
    head_owner = jnp.arange(HEADS, dtype=jnp.int32) // groups
    selector = head_owner[:, None] == jnp.arange(KV_HEADS, dtype=jnp.int32)[None, :]
    query_heads = queries.reshape(seq_count, HEADS, 1, HEAD_DIM)
    placed = jnp.where(selector[None, :, :, None], query_heads, jnp.zeros((), jnp.bfloat16))
    widened = jnp.concatenate(
        [
            placed.reshape(seq_count, HEADS, KV_HEADS * HEAD_DIM),
            jnp.zeros((seq_count, HEADS, KV_HEADS * HEAD_DIM), jnp.bfloat16),
        ],
        axis=2,
    )
    factor = HEAD_DIM ** (-0.5)
    scores = jnp.einsum("rhc,rlc->rhl", widened, paged, preferred_element_type=jnp.float32) * factor
    self_score = (
        jnp.einsum("rhc,rc->rh", widened, new_kv, preferred_element_type=jnp.float32) * factor
    )
    valid = (jnp.arange(MAXP * PAGE, dtype=jnp.int32)[None, :] < lengths[:, None])[:, None, :]
    highest = jnp.maximum(jnp.max(jnp.where(valid, scores, -1e30), axis=-1), self_score)
    expo = jnp.where(valid, jnp.exp(scores - highest[..., None]), 0.0)
    self_expo = jnp.exp(self_score - highest)
    denom = jnp.sum(expo, axis=-1) + self_expo
    probs = expo.astype(jnp.bfloat16)
    self_prob = lax.optimization_barrier(self_expo.astype(jnp.bfloat16)).astype(jnp.float32)
    mixed = jnp.einsum("rhl,rlc->rhc", probs, paged, preferred_element_type=jnp.float32)
    value_part = mixed.reshape(seq_count, HEADS, 2, KV_HEADS, HEAD_DIM)[:, :, 1]
    picked = jnp.sum(jnp.where(selector[None, :, :, None], value_part, 0.0), axis=2)
    fresh_values = new_kv.reshape(seq_count, 2, KV_HEADS, HEAD_DIM)[:, 1].astype(jnp.float32)
    fresh_picked = jnp.sum(
        jnp.where(selector[None, :, :, None], fresh_values[:, None, :, :], 0.0), axis=2
    )
    total = picked + self_prob[..., None] * fresh_picked
    return (total / denom[..., None]).astype(jnp.bfloat16).reshape(seq_count, HEADS * HEAD_DIM)


def route_slots(expert_ids):
    flat_ids = expert_ids.reshape(-1)
    onehot = (flat_ids[:, None] == jnp.arange(EXPERTS, dtype=jnp.int32)[None, :]).astype(jnp.int32)
    earlier = jnp.cumsum(onehot, axis=0) - onehot
    return (flat_ids, jnp.sum(earlier * onehot, axis=1))


def on_device(
    queries,
    kv_cache,
    new_kv,
    lengths,
    page_table,
    hidden,
    norm_gain,
    route_ids,
    route_weights,
    gate_w,
    up_w,
    down_w,
):
    context = attend_block(queries, kv_cache, page_table, lengths, new_kv)
    seq_count = hidden.shape[0]
    wide = hidden.astype(jnp.float32)
    normed = (
        wide * lax.rsqrt(jnp.mean(wide * wide, axis=-1, keepdims=True) + eps) * norm_gain
    ).astype(jnp.bfloat16)
    weights = route_weights / jnp.sum(route_weights, axis=-1, keepdims=True)
    flat_ids, ranks = route_slots(route_ids)
    column_count = gate_w.shape[1]
    split_count = max(FF // column_count, 1)
    per_device = max(column_count // FF, 1)
    unit_count = min(column_count, FF)
    device_count = lax.axis_size(("side", "dev"))
    route_count = seq_count * TOP
    portions = jnp.arange(split_count, dtype=jnp.int32)[None, :]
    target = ((flat_ids[:, None] * split_count + portions) * MOST + ranks[:, None]).reshape(-1)
    source_token = jnp.broadcast_to(
        (jnp.arange(route_count, dtype=jnp.int32) // TOP)[:, None], (route_count, split_count)
    ).reshape(-1)
    slot_source = (
        jnp.full((EXPERTS * split_count * MOST,), seq_count, jnp.int32).at[target].set(source_token)
    )
    outgoing = jnp.take(normed, slot_source, axis=0, mode="fill", fill_value=0)
    outgoing = outgoing.reshape(device_count, per_device, MOST, D)
    gate_local = gate_w.reshape(D, per_device, unit_count)
    up_local = up_w.reshape(D, per_device, unit_count)
    down_local = down_w.reshape(per_device, unit_count, D)
    arrived = lax.all_to_all(outgoing, ("side", "dev"), split_axis=0, concat_axis=0, tiled=True)
    gate_val = jnp.einsum("sejd,deh->sejh", arrived, gate_local, preferred_element_type=jnp.float32)
    up_val = jnp.einsum("sejd,deh->sejh", arrived, up_local, preferred_element_type=jnp.float32)
    activation = (jax.nn.silu(gate_val) * up_val).astype(jnp.bfloat16)
    returned = lax.all_to_all(
        jnp.einsum(
            "sejh,ehd->sejd", activation, down_local, preferred_element_type=jnp.float32
        ).astype(jnp.bfloat16),
        ("side", "dev"),
        split_axis=0,
        concat_axis=0,
        tiled=True,
    )
    returned = returned.reshape(EXPERTS * split_count * MOST, D)
    summed = returned[target].reshape(route_count, split_count, D).astype(jnp.float32).sum(axis=1)
    moe_out = jnp.sum(summed.reshape(seq_count, TOP, D) * weights[:, :, None], axis=1).astype(
        jnp.bfloat16
    )
    return (context, moe_out)


def solution(mesh):
    placed = (
        P(("groups", "side", "dev"), None),
        P(("groups", "side", "dev"), None, None),
        P(("groups", "side", "dev"), None),
        P(("groups", "side", "dev")),
        P(("groups", "side", "dev"), None),
        P(("groups", "side", "dev"), None),
        P(),
        P(("groups", "side", "dev"), None),
        P(("groups", "side", "dev"), None),
        P(None, ("side", "dev")),
        P(None, ("side", "dev")),
        P(("side", "dev"), None),
    )
    return jax.shard_map(
        on_device,
        mesh=mesh,
        in_specs=placed,
        out_specs=(P(("groups", "side", "dev"), None), P(("groups", "side", "dev"), None)),
        check_vma=False,
    )
```

profile of v0, /device:TPU:0, one launch (start us, length us, event | category | flops | bytes accessed | tf_op | source)
XLA Modules:
  0.0 218.5 jit_solution(2697544139789788821)
XLA Ops:
  0.6 0.9 eq.47
  1.5 0.7 broadcast_multiply_fusion
  2.2 0.1 fusion.46
  2.3 0.1 reduce_window_sum.11
  2.4 0.2 select_reduce_fusion.2
  2.6 0.1 mul.83
  2.7 0.8 scatter_custom_fusion
  3.5 1.0 fusion.41
  4.5 0.9 fusion.43
  5.4 1.2 gather_fusion.1
  6.6 1.2 gather.14
  7.8 0.1 broadcast_in_dim.139
  8.0 2.7 %broadcast_select_fusion = bf16[16,2,4,4096]{3,2,1,0:T(4,128)(2,1)} fusion(bf16[16,2,4,4096]{3,2,1,0:T(4,128)(2,1)} %gather.14, pred[16,2,4]{2,1,0:T(4,128)(4,1)S(1)} %broadcast_in_dim.139), kind=kLoop, calls=%fused_computation.24 | loop fusion | flops 524288 | bytes 2097280 | tf_op jit(solution)/shard_map/jit(_take)/select_n | solution.py:103
  10.7 7.4 %all-to-all-start = ((bf16[16,2,4,4096]{3,2,1,0:T(4,128)(2,1)}), bf16[16,2,4,4096]{3,2,1,0:T(4,128)(2,1)S(1)}, u32[]{:S(2)}, u32[]{:S(2)}) async-start(bf16[16,2,4,4096]{3,2,1,0:T(4,128)(2,1)} %broadcast_select_fusion), calls=%async_computation | async-start | bytes 2097152 | tf_op jit(solution)/shard_map/all_to_all | solution.py:108
  18.1 0.1 iota_compare_fusion.1
  18.2 0.1 broadcast_in_dim.124
  18.3 0.6 copy.72
  19.0 0.9 copy.28
  19.9 0.1 broadcast_in_dim.128
  20.0 0.2 broadcast_in_dim.129
  20.2 0.7 compare_select_fusion
  20.9 0.1 reshape.173
  21.0 55.1 %reshape.165 = bf16[4096,2,1536]{2,1,0:T(2,128)(2,1)} reshape(bf16[4096,3072]{1,0:T(8,128)(2,1)} %param.21) | data formatting | bytes 50331648 | tf_op jit(solution)/shard_map/reshape | solution.py:105
  76.1 55.1 %reshape.166 = bf16[4096,2,1536]{2,1,0:T(2,128)(2,1)} reshape(bf16[4096,3072]{1,0:T(8,128)(2,1)} %param.22) | data formatting | bytes 50331648 | tf_op jit(solution)/shard_map/reshape | solution.py:106
  131.2 2.9 %gather_fusion = bf16[128,16,1024]{2,1,0:T(8,128)(2,1)} fusion(bf16[44,16,1024]{2,1,0:T(8,128)(2,1)S(1)} %copy-done, s32[1024]{0:T(1024)S(1)} %pad_clamp_fusion.2), kind=kCustom, calls=%fused_computation | custom fusion | bytes 8389120 | tf_op jit(solution)/shard_map/gather | solution.py:25
  134.1 0.1 iota_compare_fusion.2
  134.2 0.3 fusion.19
  134.5 3.7 %select_reduce_fusion.1 = (f32[8,64]{1,0:T(8,128)S(1)}, f32[8,64,256]{2,1,0:T(8,128)S(1)}) fusion(pred[8,256]{1,0:T(8,128)(4,1)S(1)} %iota_compare_fusion.2, bf16[8,256,1024]{2,1,0:T(8,128)(2,1)} %bitcast.59, bf16[8,64,512]{2,1,0:T(8,128)(2,1)S(1)} %broadcast_select_fusion.1), kind=kOutput, calls=%fused_computation.33 | convolution fusion | flops 268828160 | bytes 5246976 | tf_op jit(solution)/shard_map/rhc,rlc->rhl/dot_general | solution.py:38
  138.2 17.3 %fusion.5 = f32[16,2,4,1536]{3,0,2,1:T(8,128)} fusion(bf16[4096,2,1536,1]{2,1,0,3:T(2,128)(2,1)} %bitcast.62, bf16[16,2,4,4096]{3,2,1,0:T(4,128)(2,1)S(1)} %all-to-all-done), kind=kOutput, calls=%fused_computation.10 | convolution fusion | flops 1610612736 | bytes 27000832 | tf_op jit(solution)/shard_map/sejd,deh->sejh/dot_general | solution.py:109
  155.5 24.1 %fusion.4 = bf16[16,2,4,4096]{3,0,2,1:T(8,128)(2,1)} fusion(bf16[2,1536,4096,1]{2,1,3,0:T(8,128)(2,1)} %bitcast.71, bf16[4096,2,1536,1]{2,1,0,3:T(2,128)(2,1)} %bitcast.61, bf16[16,2,4,4096]{3,2,1,0:T(4,128)(2,1)S(1)} %all-to-all-done, f32[16,2,4,1536]{3,0,2,1:T(8,128)} %fusion.5), kind=kOutput, calls=%fused_computation.9 | convolution fusion | flops 3222929408 | bytes 53215232 | tf_op jit(solution)/shard_map/sejh,ehd->sejd/dot_general | solution.py:113
  179.6 3.0 %copy.35 = bf16[16,2,4,4096]{3,2,1,0:T(4,128)(2,1)} copy(bf16[16,2,4,4096]{3,0,2,1:T(8,128)(2,1)} %fusion.4) | data formatting | bytes 2097152 | tf_op jit(solution)/shard_map/convert_element_type | solution.py:115
  182.6 6.0 %all-to-all-start.1 = ((bf16[16,2,4,4096]{3,2,1,0:T(4,128)(2,1)}), bf16[16,2,4,4096]{3,2,1,0:T(4,128)(2,1)}, u32[]{:S(2)}, u32[]{:S(2)}) async-start(bf16[16,2,4,4096]{3,2,1,0:T(4,128)(2,1)} %copy.35), calls=%async_computation.1 | async-start | bytes 2097152 | tf_op jit(solution)/shard_map/all_to_all | solution.py:112
  188.7 0.3 fusion.33
  188.9 0.6 fusion.49
  189.5 0.6 convert_element_type.50
  190.1 3.2 %fusion.36 = f32[8,64,1024]{2,1,0:T(8,128)S(1)} fusion(bf16[8,256,1024]{2,1,0:T(8,128)(2,1)} %bitcast.60, f32[8,64,256]{2,1,0:T(8,128)} %copy-done.2, f32[8,64]{1,0:T(8,128)S(1)} %multiply_maximum_fusion, pred[8,256]{1,0:T(8,128)(4,1)S(1)} %iota_compare_fusion.2), kind=kOutput, calls=%fused_computation.38 | convolution fusion | flops 268828672 | bytes 6819840 | tf_op jit(solution)/shard_map/rhl,rlc->rhc/dot_general | solution.py:49
  193.4 2.1 reshape.163
  195.4 0.7 fusion.47
  196.2 2.7 %select_reduce_fusion = (f32[8,64,128]{2,1,0:T(8,128)S(1)}, f32[8,64,128]{2,1,0:T(8,128)S(1)}) fusion(f32[8,4,128]{2,1,0:T(4,128)S(1)} %copy.30, pred[64,4]{1,0:T(8,128)(4,1)S(1)} %iota_compare_fusion.1, f32[8,64,2,4,128]{4,3,2,1,0:T(4,128)} %reshape.163), kind=kLoop, calls=%fused_computation.23 | loop fusion | flops 917504 | bytes 1589504 | tf_op jit(solution)/shard_map/reduce_sum | solution.py:53
  198.8 0.9 fusion.44
  199.8 0.7 copy.71
  200.5 0.1 reduce_sum.75
  200.6 0.6 pad_clamp_fusion
  201.2 0.1 broadcast_divide_fusion
  201.3 13.9 %all-to-all-done.1 = bf16[16,2,4,4096]{3,2,1,0:T(4,128)(2,1)} async-done(((bf16[16,2,4,4096]{3,2,1,0:T(4,128)(2,1)}), bf16[16,2,4,4096]{3,2,1,0:T(4,128)(2,1)}, u32[]{:S(2)}, u32[]{:S(2)}) %all-to-all-start.1) | async-done | bytes 1048608 | tf_op jit(solution)/shard_map/all_to_all | solution.py:112
  215.2 1.3 reshape.168
  216.5 0.9 gather_fusion.2
  217.4 1.1 fusion.24
  (28 shorter events, 0.1 us)
Async XLA Ops:
  0.6 130.6 %copy-start = (bf16[44,16,1024]{2,1,0:T(8,128)(2,1)S(1)}, bf16[44,16,1024]{2,1,0:T(8,128)(2,1)}, u32[]{:S(2)}) copy-start(bf16[44,16,1024]{2,1,0:T(8,128)(2,1)} %param.13) | copy-start | bytes 4325380
  2.7 1.8 copy-start.7
  10.7 127.5 %all-to-all-start = ((bf16[16,2,4,4096]{3,2,1,0:T(4,128)(2,1)}), bf16[16,2,4,4096]{3,2,1,0:T(4,128)(2,1)S(1)}, u32[]{:S(2)}, u32[]{:S(2)}) async-start(bf16[16,2,4,4096]{3,2,1,0:T(4,128)(2,1)} %broadcast_select_fusion), calls=%async_computation | async-start | bytes 2097152 | tf_op jit(solution)/shard_map/all_to_all | solution.py:108
  76.1 58.0 %copy-start.6 = (s32[8]{0:T(128)S(1)}, s32[8]{0:T(128)}, u32[]{:S(2)}) copy-start(s32[8]{0:T(128)} %param.15) | copy-start | bytes 100
  76.1 58.1 %copy-start.3 = (pred[8,8,4,128]{3,1,2,0:T(8,128)(4,1)S(1)}, pred[8,8,4,128]{3,1,2,0:T(8,128)(4,1)}, u32[]{:S(2)}) copy-start(pred[8,8,4,128]{3,1,2,0:T(8,128)(4,1)} %copy.72) | copy-start | bytes 98308
  76.1 58.1 %copy-start.5 = (bf16[8,1024]{1,0:T(8,128)(2,1)S(1)}, bf16[8,1024]{1,0:T(8,128)(2,1)}, u32[]{:S(2)}) copy-start(bf16[8,1024]{1,0:T(8,128)(2,1)} %param.14) | copy-start | bytes 49156
  138.2 50.5 %copy-start.2 = (f32[8,64,256]{2,1,0:T(8,128)}, f32[8,64,256]{2,1,0:T(8,128)S(1)}, u32[]{:S(2)}) copy-start(f32[8,64,256]{2,1,0:T(8,128)S(1)} %get-tuple-element.7) | copy-start | bytes 1572868
  155.5 45.0 %copy-start.4 = (f32[8,8]{1,0:T(8,128)S(1)}, f32[8,8]{1,0:T(8,128)}, u32[]{:S(2)}) copy-start(f32[8,8]{1,0:T(8,128)} %param.20) | copy-start | bytes 772
  155.5 63.0 %copy-start.1 = (bf16[44,16,1024]{2,1,0:T(8,128)(2,1)S(1)}, bf16[44,16,1024]{2,1,0:T(8,128)(2,1)}, u32[]{:S(2)}) copy-start(bf16[44,16,1024]{2,1,0:T(8,128)(2,1)} %param.13) | copy-start | bytes 4325380
  182.6 32.6 %all-to-all-start.1 = ((bf16[16,2,4,4096]{3,2,1,0:T(4,128)(2,1)}), bf16[16,2,4,4096]{3,2,1,0:T(4,128)(2,1)}, u32[]{:S(2)}, u32[]{:S(2)}) async-start(bf16[16,2,4,4096]{3,2,1,0:T(4,128)(2,1)} %copy.35), calls=%async_computation.1 | async-start | bytes 2097152 | tf_op jit(solution)/shard_map/all_to_all | solution.py:112
where the time goes:
time: 222 us; the launch traced here: 218 us
  local copies, waits for them, and re-layouts  127 us (57%)
  matrix products  48.6 us (22%)
  other arithmetic  14.3 us (6%)
  waiting for transfers between devices  13.9 us (6%)
  starting transfers between devices  13.4 us (6%)
    reshape x1, local copies, waits for them, and re-layouts, on_device(): up_local = up_w.reshape(D, per_device, unit_count)  55.1 us
    reshape x1, local copies, waits for them, and re-layouts, on_device(): gate_local = gate_w.reshape(D, per_device, unit_count)  55.1 us
    dot_general x1, matrix products, on_device(): jnp.einsum('sejh,ehd->sejd', activation, down_local, preferred_element_ty...  24.1 us
    dot_general x1, matrix products, on_device(): jnp.einsum('sejd,deh->sejh', arrived, gate_local, preferred_element_type=...  17.3 us
    all_to_all x1, waiting for transfers between devices, on_device(): lax.all_to_all(jnp.einsum('sejh,ehd->sejd', activation, down_local, prefe...  13.9 us
    all_to_all x1, starting transfers between devices, on_device(): lax.all_to_all(outgoing, ('side', 'dev'), split_axis=0, concat_axis=0, ti...  7.39 us
    all_to_all x1, starting transfers between devices, on_device(): lax.all_to_all(jnp.einsum('sejh,ehd->sejd', activation, down_local, prefe...  6.04 us
  transfers between devices with their start and end apart: 2, of which 1 were waited for; matrix products, arithmetic and copies ran while one was open for 61% of the time, Pallas kernels for 0%

commit v1 on v0

v1 whole, which is shorter than its diff:
```python
import functools

import jax
import jax.numpy as jnp
from jax import lax
from jax.experimental import pallas as pl
from jax.experimental.pallas import tpu as pltpu
from jax.sharding import PartitionSpec as P

FF = 1536
HEADS = 64
KV_HEADS = 4
HEAD_DIM = 128
EXPERTS = 32
PAGE = 16
MAXP = 16
GROUP = HEADS // KV_HEADS
AXES = ("side", "dev")
eps = 1e-06


def attend(q_ref, kv_ref, new_ref, len_ref, table_ref, out_ref):
    seqs = q_ref.shape[0]
    positions = kv_ref.shape[0]
    where = lax.broadcasted_iota(jnp.int32, (seqs, positions), 1)
    page, offset = where >> 4, where & 15
    lengths = len_ref[...]
    table = table_ref[...]
    valid = jnp.zeros((seqs, positions), jnp.int32)
    for j in range(MAXP):
        hit = (table[:, j : j + 1] == page) & (offset + j * PAGE < lengths)
        valid = valid | hit.astype(jnp.int32)
    bias = jnp.where(valid > 0, 0.0, -1e30)[:, None, :]
    valid3 = jnp.broadcast_to(bias, (seqs, GROUP, positions)) == 0.0
    factor = HEAD_DIM ** (-0.5)
    for g in range(KV_HEADS):
        cols = slice(g * HEAD_DIM, (g + 1) * HEAD_DIM)
        vcols = slice((KV_HEADS + g) * HEAD_DIM, (KV_HEADS + g + 1) * HEAD_DIM)
        q3 = q_ref[:, g * GROUP : (g + 1) * GROUP, :]
        scores = lax.dot_general(
            q3.reshape(seqs * GROUP, HEAD_DIM),
            kv_ref[:, cols],
            (((1,), (1,)), ((), ())),
            preferred_element_type=jnp.float32,
        ).reshape(seqs, GROUP, positions)
        scores = jnp.where(valid3, scores * factor, -1e30)
        own = new_ref[:, cols].astype(jnp.float32)[:, None, :]
        self_score = jnp.sum(q3.astype(jnp.float32) * own, axis=-1, keepdims=True) * factor
        highest = jnp.maximum(jnp.max(scores, axis=-1, keepdims=True), self_score)
        expo = jnp.exp(scores - highest)
        self_expo = jnp.exp(self_score - highest)
        denom = jnp.sum(expo, axis=-1, keepdims=True) + self_expo
        mixed = jnp.dot(
            expo.astype(jnp.bfloat16).reshape(seqs * GROUP, positions),
            kv_ref[:, vcols],
            preferred_element_type=jnp.float32,
        ).reshape(seqs, GROUP, HEAD_DIM)
        fresh = new_ref[:, vcols].astype(jnp.float32)[:, None, :]
        total = mixed + self_expo.astype(jnp.bfloat16).astype(jnp.float32) * fresh
        out_ref[:, g * GROUP : (g + 1) * GROUP, :] = (total / denom).astype(jnp.bfloat16)


def experts(x_ref, g_ref, gate_ref, up_ref, down_ref, out_ref, total):
    step = pl.program_id(0)

    @pl.when(step == 0)
    def _():
        total[...] = jnp.zeros_like(total)

    x = x_ref[...]
    gate = jnp.dot(x, gate_ref[...], preferred_element_type=jnp.float32)
    up = jnp.dot(x, up_ref[...], preferred_element_type=jnp.float32)
    act = (gate / (1.0 + jnp.exp(-gate)) * up).astype(jnp.bfloat16)
    total[...] += g_ref[0] * jnp.dot(act, down_ref[...], preferred_element_type=jnp.float32)

    @pl.when(step == pl.num_programs(0) - 1)
    def _():
        out_ref[...] = total[...].astype(jnp.bfloat16)


def on_device(
    queries,
    kv_cache,
    new_kv,
    lengths,
    page_table,
    hidden,
    norm_gain,
    route_ids,
    route_weights,
    gate_w,
    up_w,
    down_w,
):
    seqs, depth = hidden.shape
    wide = hidden.astype(jnp.float32)
    normed = (
        wide * lax.rsqrt(jnp.mean(wide * wide, axis=-1, keepdims=True) + eps) * norm_gain
    ).astype(jnp.bfloat16)
    weights = route_weights / jnp.sum(route_weights, axis=-1, keepdims=True)
    dense = jnp.sum(
        jnp.where(
            route_ids[:, :, None] == jnp.arange(EXPERTS, dtype=jnp.int32), weights[:, :, None], 0.0
        ),
        axis=1,
    )
    tokens = lax.all_gather(normed, AXES, axis=0, tiled=True)
    gates = lax.all_gather(dense, AXES, axis=0, tiled=True)

    positions = kv_cache.shape[0] * PAGE
    context = pl.pallas_call(
        attend,
        out_shape=jax.ShapeDtypeStruct((seqs, HEADS, HEAD_DIM), jnp.bfloat16),
        compiler_params=pltpu.CompilerParams(vmem_limit_bytes=32 << 20),
        cost_estimate=pl.CostEstimate(flops=400_000_000, bytes_accessed=2_000_000, transcendentals=400_000),
    )(
        queries.reshape(seqs, HEADS, HEAD_DIM),
        kv_cache.reshape(positions, -1),
        new_kv,
        lengths.reshape(seqs, 1),
        page_table,
    ).reshape(seqs, HEADS * HEAD_DIM)

    columns = gate_w.shape[1]
    units = min(columns, FF)
    per_device = max(columns // FF, 1)
    device = lax.axis_index(AXES)
    count = tokens.shape[0]
    mine = lax.dynamic_slice(gates, (0, device * columns // FF), (count, per_device))
    mine = mine.T.reshape(per_device, count, 1)
    tile = 256 if units % 256 == 0 else 128
    per_expert = units // tile
    part = pl.pallas_call(
        experts,
        out_shape=jax.ShapeDtypeStruct((count, depth), jnp.bfloat16),
        grid=(columns // tile,),
        in_specs=[
            pl.BlockSpec((count, depth), lambda i: (0, 0)),
            pl.BlockSpec((1, count, 1), lambda i: (i // per_expert, 0, 0)),
            pl.BlockSpec((depth, tile), lambda i: (0, i)),
            pl.BlockSpec((depth, tile), lambda i: (0, i)),
            pl.BlockSpec((tile, depth), lambda i: (i, 0)),
        ],
        out_specs=pl.BlockSpec((count, depth), lambda i: (0, 0)),
        scratch_shapes=[pltpu.VMEM((count, depth), jnp.float32)],
        compiler_params=pltpu.CompilerParams(vmem_limit_bytes=60 << 20),
    )(tokens, mine, gate_w, up_w, down_w)

    devices = lax.axis_size(AXES)
    back = lax.all_to_all(
        part.reshape(devices, seqs, depth), AXES, split_axis=0, concat_axis=0, tiled=True
    )
    moe_out = jnp.sum(back.astype(jnp.float32), axis=0).astype(jnp.bfloat16)
    return (context, moe_out)


def solution(mesh):
    rows = P(("groups", "side", "dev"), None)
    placed = (
        rows,
        P(("groups", "side", "dev"), None, None),
        rows,
        P(("groups", "side", "dev")),
        rows,
        rows,
        P(),
        rows,
        rows,
        P(None, ("side", "dev")),
        P(None, ("side", "dev")),
        P(("side", "dev"), None),
    )
    return jax.shard_map(
        on_device, mesh=mesh, in_specs=placed, out_specs=(rows, rows), check_vma=False
    )
```

time: 222 us -> 119 us (0.54); the launches traced: 218 us -> 118 us
  local copies, waits for them, and re-layouts: 127 us -> 2.53 us
  matrix products: 48.6 us -> 0 us
  blocking collectives: 0 us -> 34.6 us
  Pallas kernels: 0 us -> 30.7 us
  between operations: 0.87 us -> 14.1 us
  waiting for transfers between devices: 13.9 us -> 26.9 us
  starting transfers between devices: 13.4 us -> 3.73 us
  other arithmetic: 14.3 us -> 5.67 us
    reshape x4 -> x3, local copies, waits for them, and re-layouts: 114 us -> 1.74 us  [the longest x2 1.66 us: on_device(): mine = mine.T.reshape(per_device, count, 1)]
    dot_general x5 -> x0, matrix products: 48.6 us -> none  [the longest x1 24.1 us: on_device(): jnp.einsum('sejh,ehd->sejd', activation, down_local, preferred_element_ty...]
    all_gather x0 -> x1, blocking collectives: none -> 34.6 us  [on_device(): gates = lax.all_gather(dense, AXES, axis=0, tiled=True)]
    pallas_call x0 -> x2, Pallas kernels: none -> 30.7 us  [the longest x1 29.1 us: on_device(): pl.pallas_call(experts, out_shape=jax.ShapeDtypeStruct((count, depth), jn...]
    all_to_all x2 -> x1, waiting for transfers between devices: 13.9 us -> 23.9 us  [on_device(): lax.all_to_all(part.reshape(devices, seqs, depth), AXES, split_axis=0, co...]
    all_to_all x2 -> x1, starting transfers between devices: 13.4 us -> 3.7 us  [on_device(): lax.all_to_all(part.reshape(devices, seqs, depth), AXES, split_axis=0, co...]
    gather x4 -> x0, local copies, waits for them, and re-layouts: 6.13 us -> none  [the longest x1 2.85 us: attend_block(): paged = cache_pool[page_table].reshape(seq_count, MAXP * PAGE, width_kv)]
    select_n x7 -> x0, other arithmetic: 3.48 us -> none  [the longest x2 2.74 us: on_device(): outgoing = jnp.take(normed, slot_source, axis=0, mode='fill', fill_value=0)]
  transfers between devices with their start and end apart: 2 -> 2, of which waited for: 1 -> 2; matrix products, arithmetic and copies ran while one was open for 61% -> 4% of each run, Pallas kernels for 0% -> 1%
where the time goes in v1:
time: 119 us; the launch traced here: 118 us
  blocking collectives  34.6 us (29%)
  Pallas kernels  30.7 us (26%)
  waiting for transfers between devices  26.9 us (23%)
  between operations  14.1 us (12%)
  other arithmetic  5.67 us (5%)
  starting transfers between devices  3.73 us (3%)
  local copies, waits for them, and re-layouts  2.53 us (2%)
    all_gather x1, blocking collectives, on_device(): gates = lax.all_gather(dense, AXES, axis=0, tiled=True)  34.6 us
    pallas_call x1, Pallas kernels, on_device(): pl.pallas_call(experts, out_shape=jax.ShapeDtypeStruct((count, depth), jn...  29.1 us
    all_to_all x1, waiting for transfers between devices, on_device(): lax.all_to_all(part.reshape(devices, seqs, depth), AXES, split_axis=0, co...  23.9 us
    all_to_all x1, starting transfers between devices, on_device(): lax.all_to_all(part.reshape(devices, seqs, depth), AXES, split_axis=0, co...  3.7 us
    all_gather x1, waiting for transfers between devices, on_device(): tokens = lax.all_gather(normed, AXES, axis=0, tiled=True)  3 us
  transfers between devices with their start and end apart: 2, of which 2 were waited for; matrix products, arithmetic and copies ran while one was open for 4% of the time, Pallas kernels for 1%

profile of v1, /device:TPU:0, one launch (start us, length us, event | category | flops | bytes accessed | tf_op | source)
XLA Modules:
  0.0 118.3 jit_solution(15045162732612878560)
XLA Ops:
  7.2 0.0 all-gather.2.cloned.1.call-start
  7.2 1.0 fusion
  8.2 1.6 %fusion.2 = bf16[8,4096]{1,0:T(8,128)(2,1)} fusion(bf16[8,4096]{1,0:T(8,128)(2,1)} %param.17, f32[4096]{0:T(1024)} %param.18, f32[8]{0:T(128)S(1)} %add_rsqrt_fusion), kind=kLoop, calls=%fused_computation.4 | loop fusion | flops 131072 | bytes 147488 | tf_op jit(solution)/shard_map/convert_element_type | solution.py:99
  9.8 0.0 all-gather.2.cloned.1.call-update
  9.8 0.8 reduce_sum.40
  10.6 0.8 broadcast_divide_fusion
  11.4 0.8 select_reduce_fusion
  12.2 34.6 %all_gather.7 = f32[128,32]{1,0:T(8,128)S(1)} all-gather(f32[8,32]{1,0:T(8,128)S(1)} %select_reduce_fusion), channel_id=1, replica_groups=mesh['groups'=2,'side'=2,'dev'=8] {'side','dev'}, dimensions={0}, use_global_device_ids=true | all-gather | bytes 17408 | tf_op jit(solution)/shard_map/all_gather | solution.py:108
  46.8 0.1 dynamic-slice_bitcast_fusion
  46.9 1.6 %copy.22.g_ref = f32[2,128,1]{2,1,0:T(8,128)} copy(f32[2,128,1]{0,1,2:T(8,128)S(1)} %dynamic-slice_bitcast_fusion) | data formatting | bytes 2048 | tf_op jit(solution)/shard_map/reshape | solution.py:130
  48.5 0.0 copy-start.3
  48.5 0.0 copy-start.4
  48.5 0.0 copy-start
  48.5 0.0 copy-start.1
  48.5 0.0 copy-start.2
  48.5 3.0 %all-gather.2.cloned.1.call-done.x_ref = bf16[128,4096]{1,0:T(8,128)(2,1)} async-done(((bf16[8,4096]{1,0:T(8,128)(2,1)}), bf16[128,4096]{1,0:T(8,128)(2,1)}) %all-gather.2.cloned.1.call-update) | async-done | bytes 1048592 | tf_op jit(solution)/shard_map/all_gather | solution.py:107
  51.5 29.1 %shard_map.132 = bf16[128,4096]{1,0:T(8,128)(2,1)} custom-call(bf16[128,4096]{1,0:T(8,128)(2,1)} %all-gather.2.cloned.1.call-done.x_ref, f32[2,128,1]{2,1,0:T(8,128)} %copy.22.g_ref, bf16[4096,3072]{1,0:T(8,128)(2,1)} %gate_ref.1, bf16[4096,3072]{1,0:T(8,128)(2,1)} %up_ref.1, bf16[3072,4096]{1,0:T(8,128)(2,1)} %down_ref.1), custom_call_target="tpu_custom_call" | custom-call | tf_op jit(solution)/shard_map/pallas_call | solution.py:133
  80.5 3.7 %all-to-all-start = ((bf16[16,8,4096]{2,1,0:T(8,128)(2,1)}), bf16[16,8,4096]{2,1,0:T(8,128)(2,1)S(1)}, u32[]{:S(2)}, u32[]{:S(2)}) async-start(bf16[16,8,4096]{2,1,0:T(8,128)(2,1)} %bitcast.18), calls=%async_computation | async-start | bytes 2097152 | tf_op jit(solution)/shard_map/all_to_all | solution.py:150
  84.2 0.0 copy-done.3
  84.3 0.0 copy-done.4
  84.3 0.1 copy.20.len_ref
  84.4 0.0 copy-done
  84.4 0.0 copy-done.1
  84.4 0.0 copy-done.2
  84.4 1.7 %shard_map.131 = bf16[8,64,128]{2,1,0:T(8,128)(2,1)S(1)} custom-call(bf16[8,64,128]{2,1,0:T(8,128)(2,1)S(1)} %bitcast.17, bf16[704,1024]{1,0:T(8,128)(2,1)S(1)} %bitcast.15, bf16[8,1024]{1,0:T(8,128)(2,1)S(1)} %copy-done.1, s32[8,1]{1,0:T(8,128)S(1)} %copy.20.len_ref, s32[8,16]{1,0:T(8,128)S(1)} %copy-done.2), custom_call_target="tpu_custom_call" | custom-call | flops 400000000 | bytes 2000000 | tf_op jit(solution)/shard_map/pallas_call | solution.py:111
  86.1 0.7 copy.29
  86.8 23.9 %all-to-all-done = bf16[16,8,4096]{2,1,0:T(8,128)(2,1)S(1)} async-done(((bf16[16,8,4096]{2,1,0:T(8,128)(2,1)}), bf16[16,8,4096]{2,1,0:T(8,128)(2,1)S(1)}, u32[]{:S(2)}, u32[]{:S(2)}) %all-to-all-start) | async-done | bytes 1048608 | tf_op jit(solution)/shard_map/all_to_all | solution.py:150
  110.7 0.8 reduce_sum.42
  (2 shorter events, 0.0 us)
Async XLA Ops:
  7.2 44.3 %all-gather.2.cloned.1.call-start = ((), (), s32[]{:S(2)}) async-start(), calls=%async_computation.1 | async-start | bytes 1114112 | tf_op jit(solution)/shard_map/all_gather | solution.py:107
  48.5 35.8 %copy-start.3 = (bf16[8,8192]{1,0:T(8,128)(2,1)S(1)}, bf16[8,8192]{1,0:T(8,128)(2,1)}, u32[]{:S(2)}) copy-start(bf16[8,8192]{1,0:T(8,128)(2,1)} %param.12) | copy-start | bytes 393220
  48.5 35.8 %copy-start.4 = (s32[8]{0:T(128)S(1)}, s32[8]{0:T(128)}, u32[]{:S(2)}) copy-start(s32[8]{0:T(128)} %param.15) | copy-start | bytes 100
  48.5 35.9 %copy-start = (bf16[44,16,1024]{2,1,0:T(8,128)(2,1)S(1)}, bf16[44,16,1024]{2,1,0:T(8,128)(2,1)}, u32[]{:S(2)}) copy-start(bf16[44,16,1024]{2,1,0:T(8,128)(2,1)} %param.13) | copy-start | bytes 4325380
  48.5 35.9 %copy-start.1 = (bf16[8,1024]{1,0:T(8,128)(2,1)S(1)}, bf16[8,1024]{1,0:T(8,128)(2,1)}, u32[]{:S(2)}) copy-start(bf16[8,1024]{1,0:T(8,128)(2,1)} %new_ref.1) | copy-start | bytes 49156
  48.5 35.9 %copy-start.2 = (s32[8,16]{1,0:T(8,128)S(1)}, s32[8,16]{1,0:T(8,128)}, u32[]{:S(2)}) copy-start(s32[8,16]{1,0:T(8,128)} %table_ref.1) | copy-start | bytes 1540
  80.5 30.2 %all-to-all-start = ((bf16[16,8,4096]{2,1,0:T(8,128)(2,1)}), bf16[16,8,4096]{2,1,0:T(8,128)(2,1)S(1)}, u32[]{:S(2)}, u32[]{:S(2)}) async-start(bf16[16,8,4096]{2,1,0:T(8,128)(2,1)} %bitcast.18), calls=%async_computation | async-start | bytes 2097152 | tf_op jit(solution)/shard_map/all_to_all | solution.py:150
Sparse Core Ops, SparseCore 0:
  10.8 40.6 all-gather.1

commit v2 on v1

v2 whole, which is shorter than its diff:
```python
import functools

import jax
import jax.numpy as jnp
from jax import lax
from jax.experimental import pallas as pl
from jax.experimental.pallas import tpu as pltpu
from jax.sharding import PartitionSpec as P

FF = 1536
HEADS = 64
KV_HEADS = 4
HEAD_DIM = 128
EXPERTS = 32
PAGE = 16
MAXP = 16
GROUP = HEADS // KV_HEADS
eps = 1e-06


def attend(q_ref, kv_ref, new_ref, len_ref, table_ref, out_ref):
    seqs = q_ref.shape[0]
    positions = kv_ref.shape[0]
    where = lax.broadcasted_iota(jnp.int32, (seqs, positions), 1)
    page, offset = where >> 4, where & 15
    lengths = len_ref[...]
    table = table_ref[...]
    valid = jnp.zeros((seqs, positions), jnp.int32)
    for j in range(MAXP):
        hit = (table[:, j : j + 1] == page) & (offset + j * PAGE < lengths)
        valid = valid | hit.astype(jnp.int32)
    bias = jnp.where(valid > 0, 0.0, -1e30)[:, None, :]
    valid3 = jnp.broadcast_to(bias, (seqs, GROUP, positions)) == 0.0
    factor = HEAD_DIM ** (-0.5)
    for g in range(KV_HEADS):
        cols = slice(g * HEAD_DIM, (g + 1) * HEAD_DIM)
        vcols = slice((KV_HEADS + g) * HEAD_DIM, (KV_HEADS + g + 1) * HEAD_DIM)
        q3 = q_ref[:, g * GROUP : (g + 1) * GROUP, :]
        scores = lax.dot_general(
            q3.reshape(seqs * GROUP, HEAD_DIM),
            kv_ref[:, cols],
            (((1,), (1,)), ((), ())),
            preferred_element_type=jnp.float32,
        ).reshape(seqs, GROUP, positions)
        scores = jnp.where(valid3, scores * factor, -1e30)
        own = new_ref[:, cols].astype(jnp.float32)[:, None, :]
        self_score = jnp.sum(q3.astype(jnp.float32) * own, axis=-1, keepdims=True) * factor
        highest = jnp.maximum(jnp.max(scores, axis=-1, keepdims=True), self_score)
        expo = jnp.exp(scores - highest)
        self_expo = jnp.exp(self_score - highest)
        denom = jnp.sum(expo, axis=-1, keepdims=True) + self_expo
        mixed = jnp.dot(
            expo.astype(jnp.bfloat16).reshape(seqs * GROUP, positions),
            kv_ref[:, vcols],
            preferred_element_type=jnp.float32,
        ).reshape(seqs, GROUP, HEAD_DIM)
        fresh = new_ref[:, vcols].astype(jnp.float32)[:, None, :]
        total = mixed + self_expo.astype(jnp.bfloat16).astype(jnp.float32) * fresh
        out_ref[:, g * GROUP : (g + 1) * GROUP, :] = (total / denom).astype(jnp.bfloat16)


def layer(
    n,
    tile,
    block,
    q_ref,
    kv_ref,
    new_ref,
    len_ref,
    table_ref,
    hid_ref,
    gain_ref,
    ids_ref,
    rw_ref,
    gate_hbm,
    up_hbm,
    down_hbm,
    ctx_ref,
    moe_ref,
    gate_buf,
    up_buf,
    down_buf,
    packed,
    x_buf,
    g_buf,
    act_buf,
    y_buf,
    half_out,
    half_in,
    z_out,
    z_in,
    gate_sem,
    up_sem,
    down_sem,
    tok_sem,
    half_sem,
    z_sem,
):
    side, me = lax.axis_index("side"), lax.axis_index("dev")
    seqs, depth = hid_ref.shape
    half = depth // 2
    columns = gate_hbm.shape[1]
    steps, slots = columns // tile, gate_buf.shape[0]
    blocks, down_slots = depth // block, down_buf.shape[0]
    per_expert = min(columns, FF) // tile
    first = (side * n + me) * columns // FF

    def fetch(i):
        slot = lax.rem(i, slots)
        cols = pl.ds(pl.multiple_of(i * tile, tile), tile)
        return (
            pltpu.make_async_copy(gate_hbm.at[:, cols], gate_buf.at[slot], gate_sem.at[slot]),
            pltpu.make_async_copy(up_hbm.at[:, cols], up_buf.at[slot], up_sem.at[slot]),
        )

    def fetch_down(c):
        slot = lax.rem(c, down_slots)
        cols = pl.ds(pl.multiple_of(c * block, block), block)
        return pltpu.make_async_copy(down_hbm.at[:, cols], down_buf.at[slot], down_sem.at[slot])

    @pl.loop(0, slots)
    def _(i):
        for copy in fetch(i):
            copy.start()

    @pl.loop(0, down_slots)
    def _(c):
        fetch_down(c).start()

    barrier = pltpu.get_barrier_semaphore()
    pl.semaphore_signal(
        barrier, inc=1, device_id={"side": 1 - side}, device_id_type=pl.DeviceIdType.MESH
    )

    @pl.loop(1, n)
    def _(k):
        pl.semaphore_signal(
            barrier,
            inc=1,
            device_id={"dev": lax.rem(me + k, n)},
            device_id_type=pl.DeviceIdType.MESH,
        )

    wide = hid_ref[...].astype(jnp.float32)
    scale = lax.rsqrt(jnp.mean(wide * wide, axis=-1, keepdims=True) + eps)
    normed = wide * scale * gain_ref[...]
    rw = rw_ref[...]
    rw = rw / jnp.sum(rw, axis=-1, keepdims=True)
    ids = ids_ref[...]
    lane = lax.broadcasted_iota(jnp.int32, (seqs, 128), 1)
    dense = jnp.zeros((seqs, 128), jnp.float32)
    for j in range(ids.shape[1]):
        dense = dense + jnp.where(ids[:, j : j + 1] == (lane & 31), rw[:, j : j + 1], 0.0)
    top = dense.astype(jnp.bfloat16).astype(jnp.float32)
    rest = dense - top
    middle = rest.astype(jnp.bfloat16).astype(jnp.float32)
    terms = jnp.where(lane < 32, top, jnp.where(lane < 64, middle, rest - middle))
    terms = jnp.where(lane < 96, terms, 0.0)
    mine = side * n + me
    packed[mine, :, :half] = jnp.concatenate([normed[:, :half], normed[:, half:]], axis=0).astype(
        jnp.bfloat16
    )
    packed[mine, :, half:] = jnp.concatenate([terms, terms], axis=0).astype(jnp.bfloat16)

    pl.semaphore_wait(barrier, n)

    @pl.loop(1, n)
    def _(k):
        pltpu.make_async_remote_copy(
            src_ref=packed.at[mine],
            dst_ref=packed.at[mine],
            send_sem=tok_sem.at[0],
            recv_sem=tok_sem.at[1],
            device_id={"dev": lax.rem(me + k, n)},
            device_id_type=pl.DeviceIdType.MESH,
        ).start()

    attend(q_ref, kv_ref, new_ref, len_ref, table_ref, ctx_ref)

    others = packed.at[pl.ds(0, n - 1)]
    pltpu.make_async_copy(others, others, tok_sem.at[1]).wait()
    own_side = packed.at[pl.ds(side * n, n)]
    swap = pltpu.make_async_remote_copy(
        src_ref=own_side,
        dst_ref=own_side,
        send_sem=tok_sem.at[2],
        recv_sem=tok_sem.at[3],
        device_id={"side": 1 - side},
        device_id_type=pl.DeviceIdType.MESH,
    )
    swap.start()
    swap.wait()
    pltpu.make_async_copy(others, others, tok_sem.at[0]).wait()

    @pl.loop(0, n)
    def _(p):
        both = packed[pl.ds(2 * p, 2)].astype(jnp.float32)
        rows = pl.ds(pl.multiple_of(p * 2 * seqs, 2 * seqs), 2 * seqs)
        low = both[:, :seqs, :half].reshape(2 * seqs, half)
        high = both[:, seqs:, :half].reshape(2 * seqs, half)
        x_buf[rows, :half] = low.astype(jnp.bfloat16)
        x_buf[rows, half:] = high.astype(jnp.bfloat16)
        g_buf[rows, :] = both[:, :seqs, half:].reshape(2 * seqs, 128)

    @pl.loop(0, steps)
    def _(i):
        slot = lax.rem(i, slots)
        for copy in fetch(i):
            copy.wait()
        x = x_buf[...]
        gate = jnp.dot(x, gate_buf[slot], preferred_element_type=jnp.float32)
        up = jnp.dot(x, up_buf[slot], preferred_element_type=jnp.float32)
        terms = g_buf[...]
        place = lax.broadcasted_iota(jnp.int32, terms.shape, 1) & 31
        share = jnp.sum(
            jnp.where(place == first + i // per_expert, terms, 0.0), axis=1, keepdims=True
        )
        act = gate / (1.0 + jnp.exp(-gate)) * up * share
        act_buf[:, pl.ds(pl.multiple_of(i * tile, tile), tile)] = act.astype(jnp.bfloat16)

        @pl.when(i + slots < steps)
        def _():
            for copy in fetch(i + slots):
                copy.start()

    def to_partner(c):
        return pltpu.make_async_remote_copy(
            src_ref=half_out.at[c],
            dst_ref=half_in.at[c],
            send_sem=half_sem.at[0, c],
            recv_sem=half_sem.at[1, c],
            device_id={"side": 1 - side},
            device_id_type=pl.DeviceIdType.MESH,
        )

    def multiply(c):
        slot = lax.rem(c, down_slots)
        fetch_down(c).wait()
        y = jnp.dot(act_buf[...], down_buf[slot], preferred_element_type=jnp.float32)
        y_buf[lax.rem(c, 2)] = y.reshape(2, n * seqs, block)
        half_out[c] = y_buf[lax.rem(c, 2), 1 - side].astype(jnp.bfloat16)
        to_partner(c).start()

        @pl.when(c + down_slots < blocks)
        def _():
            fetch_down(c + down_slots).start()

    def spread(c):
        to_partner(c).wait_recv()
        total = y_buf[lax.rem(c, 2), side] + half_in[c].astype(jnp.float32)
        total = total.reshape(n, seqs, block)
        z_out[c] = jnp.concatenate(
            [total[:, :, : block // 2], total[:, :, block // 2 :]], axis=1
        ).astype(jnp.bfloat16)

        @pl.loop(1, n)
        def _(k):
            to = lax.rem(me + k, n)
            pltpu.make_async_remote_copy(
                src_ref=z_out.at[c, to],
                dst_ref=z_in.at[c, k - 1],
                send_sem=z_sem.at[0, c],
                recv_sem=z_sem.at[1, c],
                device_id={"dev": to},
                device_id_type=pl.DeviceIdType.MESH,
            ).start()

    multiply(0)

    @pl.loop(1, blocks)
    def _(c):
        multiply(c)
        spread(c - 1)

    spread(blocks - 1)

    @pl.loop(0, blocks)
    def _(c):
        pltpu.make_async_copy(z_in.at[c], z_in.at[c], z_sem.at[1, c]).wait()
        total = jnp.sum(z_in[c].astype(jnp.float32), axis=0) + z_out[c, me].astype(jnp.float32)
        merged = jnp.concatenate([total[:seqs], total[seqs:]], axis=1)
        moe_ref[:, pl.ds(pl.multiple_of(c * block, block), block)] = merged.astype(jnp.bfloat16)
        to_partner(c).wait_send()
        pltpu.make_async_copy(z_in.at[c], z_in.at[c], z_sem.at[0, c]).wait()


def on_device(
    queries,
    kv_cache,
    new_kv,
    lengths,
    page_table,
    hidden,
    norm_gain,
    route_ids,
    route_weights,
    gate_w,
    up_w,
    down_w,
):
    seqs, depth = hidden.shape
    positions = kv_cache.shape[0] * PAGE
    columns = gate_w.shape[1]
    units = min(columns, FF)
    n = lax.axis_size("dev")
    tokens = 2 * n * seqs
    tile = 256 if units % 256 == 0 else 128
    slots = min(columns // tile, 8)
    block = 512
    blocks = depth // block
    down_slots = min(blocks, 4)
    bf16 = jnp.bfloat16
    dma = pltpu.SemaphoreType.DMA
    vmem = pl.BlockSpec(memory_space=pltpu.VMEM)
    hbm = pl.BlockSpec(memory_space=pl.ANY)
    context, moe_out = pl.pallas_call(
        functools.partial(layer, n, tile, block),
        out_shape=(
            jax.ShapeDtypeStruct((seqs, HEADS, HEAD_DIM), bf16),
            jax.ShapeDtypeStruct((seqs, depth), bf16),
        ),
        in_specs=[vmem] * 9 + [hbm] * 3,
        out_specs=(vmem, vmem),
        scratch_shapes=[
            pltpu.VMEM((slots, depth, tile), bf16),
            pltpu.VMEM((slots, depth, tile), bf16),
            pltpu.VMEM((down_slots, columns, block), bf16),
            pltpu.VMEM((2 * n, 2 * seqs, depth // 2 + 128), bf16),
            pltpu.VMEM((tokens, depth), bf16),
            pltpu.VMEM((tokens, 128), jnp.float32),
            pltpu.VMEM((tokens, columns), bf16),
            pltpu.VMEM((2, 2, n * seqs, block), jnp.float32),
            pltpu.VMEM((blocks, n * seqs, block), bf16),
            pltpu.VMEM((blocks, n * seqs, block), bf16),
            pltpu.VMEM((blocks, n, 2 * seqs, block // 2), bf16),
            pltpu.VMEM((blocks, n - 1, 2 * seqs, block // 2), bf16),
            dma((slots,)),
            dma((slots,)),
            dma((down_slots,)),
            dma((4,)),
            dma((2, blocks)),
            dma((2, blocks)),
        ],
        compiler_params=pltpu.CompilerParams(
            collective_id=0, has_side_effects=True, vmem_limit_bytes=60 << 20
        ),
        cost_estimate=pl.CostEstimate(
            flops=6 * tokens * depth * columns,
            bytes_accessed=6 * depth * columns,
            transcendentals=tokens * columns,
        ),
    )(
        queries.reshape(seqs, HEADS, HEAD_DIM),
        kv_cache.reshape(positions, -1),
        new_kv,
        lengths.reshape(seqs, 1),
        page_table,
        hidden,
        norm_gain.reshape(1, depth),
        route_ids,
        route_weights,
        gate_w,
        up_w,
        down_w,
    )
    return (context.reshape(seqs, HEADS * HEAD_DIM), moe_out)


def solution(mesh):
    rows = P(("groups", "side", "dev"), None)
    placed = (
        rows,
        P(("groups", "side", "dev"), None, None),
        rows,
        P(("groups", "side", "dev")),
        rows,
        rows,
        P(),
        rows,
        rows,
        P(None, ("side", "dev")),
        P(None, ("side", "dev")),
        P(("side", "dev"), None),
    )
    return jax.shard_map(
        on_device, mesh=mesh, in_specs=placed, out_specs=(rows, rows), check_vma=False
    )
```

time: 119 us -> 53.8 us (0.45)
  blocking collectives: 34.6 us -> 0 us
  waiting for transfers between devices: 26.9 us -> 0 us
  Pallas kernels: 30.7 us -> 46.9 us
  between operations: 14.1 us -> 0.64 us
  other arithmetic: 5.67 us -> 0 us
  starting transfers between devices: 3.73 us -> 0 us
  local copies, waits for them, and re-layouts: 2.53 us -> 6.02 us
    all_gather x1 -> x0, blocking collectives: 34.6 us -> none  [on_device(): gates = lax.all_gather(dense, AXES, axis=0, tiled=True)]
    all_to_all x1 -> x0, waiting for transfers between devices: 23.9 us -> none  [on_device(): lax.all_to_all(part.reshape(devices, seqs, depth), AXES, split_axis=0, co...]
    pallas_call x2 -> x1, Pallas kernels: 30.7 us -> 46.9 us  [on_device(): pl.pallas_call(functools.partial(layer, n, tile, block), out_shape=(jax.S...]
    unnamed x12 -> x3, local copies, waits for them, and re-layouts: 0.79 us -> 4.7 us
    all_to_all x1 -> x0, starting transfers between devices: 3.7 us -> none  [on_device(): lax.all_to_all(part.reshape(devices, seqs, depth), AXES, split_axis=0, co...]
    reduce_sum x4 -> x0, other arithmetic: 3.35 us -> none  [the longest x1 0.99 us: on_device(): jnp.mean(wide * wide, axis=-1, keepdims=True) + eps]
    all_gather x1 -> x0, waiting for transfers between devices: 3 us -> none  [on_device(): tokens = lax.all_gather(normed, AXES, axis=0, tiled=True)]
    reshape x2 -> x0, local copies, waits for them, and re-layouts: 1.66 us -> none  [on_device(): mine = mine.T.reshape(per_device, count, 1)]
  transfers between devices with their start and end apart: 2 -> 0, of which waited for: 2 -> 0; matrix products, arithmetic and copies ran while one was open for 4% -> 0% of each run, Pallas kernels for 1% -> 0%
where the time goes in v2:
time: 53.8 us; the launch traced here: 53.5 us
  Pallas kernels  46.9 us (87%)
  local copies, waits for them, and re-layouts  6.02 us (11%)
  between operations  0.64 us (1%)
    pallas_call x1, Pallas kernels, on_device(): pl.pallas_call(functools.partial(layer, n, tile, block), out_shape=(jax.S...  46.9 us
    unnamed x3, local copies, waits for them, and re-layouts  4.7 us
    reshape x1, local copies, waits for them, and re-layouts, on_device(): lengths.reshape(seqs, 1)  1.32 us

profile of v2, /device:TPU:0, one launch (start us, length us, event | category | flops | bytes accessed | tf_op | source)
XLA Modules:
  0.0 53.5 jit_solution(8726181365770601148)
XLA Ops:
  0.6 1.3 %copy.14.len_ref = s32[8,1]{1,0:T(8,128)} copy(s32[8,1]{0,1:T(1,128)} %bitcast.17) | data formatting | bytes 64 | tf_op jit(solution)/shard_map/reshape | solution.py:356
  2.0 1.6 %copy.20 = bf16[1,8,64,128]{3,2,1,0:T(8,128)(2,1)} copy(bf16[1,8,64,128]{3,1,2,0:T(8,128)(2,1)} %bitcast.13) | data formatting | bytes 262144
  3.5 46.9 %shard_map.131 = (bf16[8,64,128]{2,1,0:T(8,128)(2,1)}, bf16[8,4096]{1,0:T(8,128)(2,1)}) custom-call(bf16[8,64,128]{2,1,0:T(8,128)(2,1)} %bitcast.12, bf16[704,1024]{1,0:T(8,128)(2,1)} %bitcast.11, bf16[8,1024]{1,0:T(8,128)(2,1)} %new_ref.1, s32[8,1]{1,0:T(8,128)} %copy.14.len_ref, s32[8,16]{1,0:T(8,128)} %table_ref.1, bf16[8,4096]{1,0:T(8,128)(2,1)} %hid_ref.1, ...), custom_call_target="tpu_custom_call" | custom-call | flops 9663676416 | bytes 75497472 | tf_op jit(solution)/shard_map/pallas_call | solution.py:316
  50.4 1.6 %copy.19 = bf16[1,8,64,128]{3,1,2,0:T(8,128)(2,1)} copy(bf16[1,8,64,128]{3,2,1,0:T(8,128)(2,1)} %bitcast.15) | data formatting | bytes 262144
  52.1 1.5 %copy.22 = bf16[8,4096]{1,0:T(8,128)(2,1)} copy(bf16[8,4096]{1,0:T(8,128)(2,1)} %get-tuple-element.9) | data formatting | bytes 131072

commit v3 on v2

--- a/solution.py
+++ b/solution.py
@@ -22,41 +22,51 @@
     seqs = q_ref.shape[0]
     positions = kv_ref.shape[0]
     where = lax.broadcasted_iota(jnp.int32, (seqs, positions), 1)
+    row = lax.broadcasted_iota(jnp.int32, (seqs, positions), 0)
     page, offset = where >> 4, where & 15
-    lengths = len_ref[...]
+    lengths = jnp.zeros((seqs, positions), jnp.int32)
+    for t in range(seqs):
+        lengths = jnp.where(row == t, len_ref[t], lengths)
     table = table_ref[...]
     valid = jnp.zeros((seqs, positions), jnp.int32)
     for j in range(MAXP):
         hit = (table[:, j : j + 1] == page) & (offset + j * PAGE < lengths)
         valid = valid | hit.astype(jnp.int32)
-    bias = jnp.where(valid > 0, 0.0, -1e30)[:, None, :]
-    valid3 = jnp.broadcast_to(bias, (seqs, GROUP, positions)) == 0.0
+    valid3 = jnp.broadcast_to(valid[None], (GROUP, seqs, positions)) > 0
     factor = HEAD_DIM ** (-0.5)
     for g in range(KV_HEADS):
         cols = slice(g * HEAD_DIM, (g + 1) * HEAD_DIM)
         vcols = slice((KV_HEADS + g) * HEAD_DIM, (KV_HEADS + g + 1) * HEAD_DIM)
-        q3 = q_ref[:, g * GROUP : (g + 1) * GROUP, :]
+        heads = [
+            q_ref[:, h * HEAD_DIM : (h + 1) * HEAD_DIM].astype(jnp.float32)
+            for h in range(g * GROUP, (g + 1) * GROUP)
+        ]
+        q = jnp.concatenate(heads, axis=0)
         scores = lax.dot_general(
-            q3.reshape(seqs * GROUP, HEAD_DIM),
+            q.astype(jnp.bfloat16),
             kv_ref[:, cols],
             (((1,), (1,)), ((), ())),
             preferred_element_type=jnp.float32,
-        ).reshape(seqs, GROUP, positions)
+        ).reshape(GROUP, seqs, positions)
         scores = jnp.where(valid3, scores * factor, -1e30)
-        own = new_ref[:, cols].astype(jnp.float32)[:, None, :]
-        self_score = jnp.sum(q3.astype(jnp.float32) * own, axis=-1, keepdims=True) * factor
+        own = new_ref[:, cols].astype(jnp.float32)[None]
+        q3 = q.reshape(GROUP, seqs, HEAD_DIM)
+        self_score = jnp.sum(q3 * own, axis=-1, keepdims=True) * factor
         highest = jnp.maximum(jnp.max(scores, axis=-1, keepdims=True), self_score)
         expo = jnp.exp(scores - highest)
         self_expo = jnp.exp(self_score - highest)
         denom = jnp.sum(expo, axis=-1, keepdims=True) + self_expo
         mixed = jnp.dot(
-            expo.astype(jnp.bfloat16).reshape(seqs * GROUP, positions),
+            expo.reshape(GROUP * seqs, positions).astype(jnp.bfloat16),
             kv_ref[:, vcols],
             preferred_element_type=jnp.float32,
-        ).reshape(seqs, GROUP, HEAD_DIM)
-        fresh = new_ref[:, vcols].astype(jnp.float32)[:, None, :]
+        ).reshape(GROUP, seqs, HEAD_DIM)
+        fresh = new_ref[:, vcols].astype(jnp.float32)[None]
         total = mixed + self_expo.astype(jnp.bfloat16).astype(jnp.float32) * fresh
-        out_ref[:, g * GROUP : (g + 1) * GROUP, :] = (total / denom).astype(jnp.bfloat16)
+        total = (total / denom).astype(jnp.bfloat16)
+        for h in range(GROUP):
+            at = (g * GROUP + h) * HEAD_DIM
+            out_ref[:, at : at + HEAD_DIM] = total[h]
 
 
 def layer(
@@ -93,10 +103,15 @@
     up_sem,
     down_sem,
     tok_sem,
+    ring_sem,
     half_sem,
     z_sem,
 ):
     side, me = lax.axis_index("side"), lax.axis_index("dev")
+    ranks = n // 2
+    rank, odd = me // 2, me % 2
+    mesh_id = pl.DeviceIdType.MESH
+    partner, pair = {"side": 1 - side}, {"dev": rank * 2 + 1 - odd}
     seqs, depth = hid_ref.shape
     half = depth // 2
     columns = gate_hbm.shape[1]
@@ -129,7 +144,7 @@
 
     barrier = pltpu.get_barrier_semaphore()
     pl.semaphore_signal(
-        barrier, inc=1, device_id={"side": 1 - side}, device_id_type=pl.DeviceIdType.MESH
+        barrier, inc=1, device_id=partner, device_id_type=mesh_id
     )
 
     @pl.loop(1, n)
@@ -138,8 +153,11 @@
             barrier,
             inc=1,
             device_id={"dev": lax.rem(me + k, n)},
-            device_id_type=pl.DeviceIdType.MESH,
+            device_id_type=mesh_id,
         )
+
+    def peer(k):
+        return {"dev": lax.rem(rank + k, ranks) * 2 + odd}
 
     wide = hid_ref[...].astype(jnp.float32)
     scale = lax.rsqrt(jnp.mean(wide * wide, axis=-1, keepdims=True) + eps)
@@ -164,33 +182,52 @@
 
     pl.semaphore_wait(barrier, n)
 
-    @pl.loop(1, n)
+    @pl.loop(1, ranks)
     def _(k):
         pltpu.make_async_remote_copy(
             src_ref=packed.at[mine],
             dst_ref=packed.at[mine],
             send_sem=tok_sem.at[0],
-            recv_sem=tok_sem.at[1],
-            device_id={"dev": lax.rem(me + k, n)},
-            device_id_type=pl.DeviceIdType.MESH,
+            recv_sem=ring_sem.at[k],
+            device_id=peer(k),
+            device_id_type=mesh_id,
         ).start()
 
+    def forward(index):
+        pltpu.make_async_remote_copy(
+            src_ref=packed.at[index],
+            dst_ref=packed.at[index],
+            send_sem=tok_sem.at[1],
+            recv_sem=tok_sem.at[4],
+            device_id=pair,
+            device_id_type=mesh_id,
+        ).start()
+
+    forward(mine)
     attend(q_ref, kv_ref, new_ref, len_ref, table_ref, ctx_ref)
 
-    others = packed.at[pl.ds(0, n - 1)]
-    pltpu.make_async_copy(others, others, tok_sem.at[1]).wait()
+    @pl.loop(1, ranks)
+    def _(k):
+        index = side * n + lax.rem(rank - k + ranks, ranks) * 2 + odd
+        pltpu.make_async_copy(packed.at[index], packed.at[index], ring_sem.at[k]).wait()
+        forward(index)
+
+    others = packed.at[pl.ds(0, ranks - 1)]
+    whole = packed.at[pl.ds(0, ranks)]
+    pltpu.make_async_copy(whole, whole, tok_sem.at[4]).wait()
     own_side = packed.at[pl.ds(side * n, n)]
     swap = pltpu.make_async_remote_copy(
         src_ref=own_side,
         dst_ref=own_side,
         send_sem=tok_sem.at[2],
         recv_sem=tok_sem.at[3],
-        device_id={"side": 1 - side},
-        device_id_type=pl.DeviceIdType.MESH,
+        device_id=partner,
+        device_id_type=mesh_id,
     )
     swap.start()
     swap.wait()
     pltpu.make_async_copy(others, others, tok_sem.at[0]).wait()
+    pltpu.make_async_copy(whole, whole, tok_sem.at[1]).wait()
 
     @pl.loop(0, n)
     def _(p):
@@ -229,8 +266,8 @@
             dst_ref=half_in.at[c],
             send_sem=half_sem.at[0, c],
             recv_sem=half_sem.at[1, c],
-            device_id={"side": 1 - side},
-            device_id_type=pl.DeviceIdType.MESH,
+            device_id=partner,
+            device_id_type=mesh_id,
         )
 
     def multiply(c):
@@ -262,7 +299,7 @@
                 send_sem=z_sem.at[0, c],
                 recv_sem=z_sem.at[1, c],
                 device_id={"dev": to},
-                device_id_type=pl.DeviceIdType.MESH,
+                device_id_type=mesh_id,
             ).start()
 
     multiply(0)
@@ -303,6 +340,7 @@
     columns = gate_w.shape[1]
     units = min(columns, FF)
     n = lax.axis_size("dev")
+    ranks = n // 2
     tokens = 2 * n * seqs
     tile = 256 if units % 256 == 0 else 128
     slots = min(columns // tile, 8)
@@ -316,10 +354,10 @@
     context, moe_out = pl.pallas_call(
         functools.partial(layer, n, tile, block),
         out_shape=(
-            jax.ShapeDtypeStruct((seqs, HEADS, HEAD_DIM), bf16),
+            jax.ShapeDtypeStruct((seqs, HEADS * HEAD_DIM), bf16),
             jax.ShapeDtypeStruct((seqs, depth), bf16),
         ),
-        in_specs=[vmem] * 9 + [hbm] * 3,
+        in_specs=[vmem] * 3 + [pl.BlockSpec(memory_space=pltpu.SMEM)] + [vmem] * 5 + [hbm] * 3,
         out_specs=(vmem, vmem),
         scratch_shapes=[
             pltpu.VMEM((slots, depth, tile), bf16),
@@ -337,7 +375,8 @@
             dma((slots,)),
             dma((slots,)),
             dma((down_slots,)),
-            dma((4,)),
+            dma((5,)),
+            dma((ranks,)),
             dma((2, blocks)),
             dma((2, blocks)),
         ],
@@ -350,10 +389,10 @@
             transcendentals=tokens * columns,
         ),
     )(
-        queries.reshape(seqs, HEADS, HEAD_DIM),
+        queries,
         kv_cache.reshape(positions, -1),
         new_kv,
-        lengths.reshape(seqs, 1),
+        lengths,
         page_table,
         hidden,
         norm_gain.reshape(1, depth),
@@ -363,7 +402,7 @@
         up_w,
         down_w,
     )
-    return (context.reshape(seqs, HEADS * HEAD_DIM), moe_out)
+    return (context, moe_out)
 
 
 def solution(mesh):

time: 53.8 us -> 49 us (0.911)
  local copies, waits for them, and re-layouts: 6.02 us -> 3.04 us
  Pallas kernels: 46.9 us -> 45.1 us
    pallas_call x1, Pallas kernels: 46.9 us -> 45.1 us  [on_device(): pl.pallas_call(functools.partial(layer, n, tile, block), out_shape=(jax.S...]
    unnamed x3 -> x2, local copies, waits for them, and re-layouts: 4.7 us -> 3.04 us
    reshape x1 -> x0, local copies, waits for them, and re-layouts: 1.32 us -> none  [on_device(): lengths.reshape(seqs, 1)]
where the time goes in v3:
time: 49 us; the launch traced here: 48.8 us
  Pallas kernels  45.1 us (92%)
  local copies, waits for them, and re-layouts  3.04 us (6%)
  between operations  0.64 us (1%)
    pallas_call x1, Pallas kernels, on_device(): pl.pallas_call(functools.partial(layer, n, tile, block), out_shape=(jax.S...  45.1 us
    unnamed x2, local copies, waits for them, and re-layouts  3.04 us

profile of v3, /device:TPU:0, one launch (start us, length us, event | category | flops | bytes accessed | tf_op | source)
XLA Modules:
  0.0 48.8 jit_solution(16498781564231659089)
XLA Ops:
  0.6 45.1 %shard_map.131 = (bf16[8,8192]{1,0:T(8,128)(2,1)}, bf16[8,4096]{1,0:T(8,128)(2,1)}) custom-call(bf16[8,8192]{1,0:T(8,128)(2,1)} %q_ref.1, bf16[704,1024]{1,0:T(8,128)(2,1)} %bitcast.2, bf16[8,1024]{1,0:T(8,128)(2,1)} %new_ref.1, s32[8]{0:T(128)} %len_ref.1, s32[8,16]{1,0:T(8,128)} %table_ref.1, bf16[8,4096]{1,0:T(8,128)(2,1)} %hid_ref.1, f32[1,4096]{1,0:T(1,128)} %bitcast.3, ...), custom_call_target="tpu_custom_call" | custom-call | flops 9663676416 | bytes 75497472 | tf_op jit(solution)/shard_map/pallas_call | solution.py:354
  45.7 1.6 %copy.16 = bf16[8,8192]{1,0:T(8,128)(2,1)} copy(bf16[8,8192]{1,0:T(8,128)(2,1)} %get-tuple-element.4) | data formatting | bytes 262144
  47.3 1.5 %copy.17 = bf16[8,4096]{1,0:T(8,128)(2,1)} copy(bf16[8,4096]{1,0:T(8,128)(2,1)} %get-tuple-element.5) | data formatting | bytes 131072
